TPU v7x, 256 devices: a whole 4x4x8 slice. The times are simulated.
256 devices in a mesh: head: 16 (over z, x_hi), ctx: 16 (over y, x_lo, core).
Axes of the slice: x: 4 (x_hi: 2, x_lo: 2; x = x_hi * 2 + x_lo), y: 4, z: 8, core: 2. Of those that a mesh axis runs over, the one named last changes fastest.
Arguments:
- queries: bfloat16 [32768, 2048], P(('head', 'ctx')), may hold values from -16 to 16
- keys: bfloat16 [32768, 256], P(('head', 'ctx')), may hold values from -16 to 16
- values: bfloat16 [32768, 256], P(('head', 'ctx')), may hold values from -6 to 6
- lengths: int32 [16], replicated, may hold values from 1 to 384, 512 in all
Outputs:
- attended: bfloat16 [32768, 2048], P(('head', 'ctx'))
All inputs are finite; a program needn't handle non-finite values.
Results may differ from a plain program's by a relative error of at most 0.006.
Values may be sent and summed in bfloat16 or wider, within the bound.
No kernel may reach another device: no remote copies, remote signals or barrier semaphores. Data moves between devices by JAX's collectives and lax.ppermute only.
A program may use at most 64 MiB of HBM per device.

v0:
```python
import functools
import math

import jax
import jax.numpy as jnp
from jax import lax
from jax.experimental import pallas as pl
from jax.experimental.pallas import tpu as pltpu
from jax.sharding import Mesh, PartitionSpec as P

HD = 128
BLOCK = 64
AXES = ("z", "xh", "y", "xl", "c")
SIZES = (8, 2, 4, 2, 2)
PLANE = 4096
TILE = 128
MASKED = -2e30
FLOOR = -1e29
NEVER = 1e30
LOG2E_SCALE = math.log2(math.e) / math.sqrt(HD)
SHIFTS = (0, -1, 1, 2)
UNITS = ((8, False), (4, False), (2, False), (1, False), (1, True))
WIDEST = UNITS[0][0]


def layout(blocks):
    offsets = [len(UNITS) + 2]
    for wide, masked in UNITS:
        most = blocks if wide == 8 else 8 * 3 if masked else 8
        offsets.append(offsets[-1] + most)
    return offsets[:-1] + [offsets[-1], offsets[-1] + 8 * blocks, offsets[-1] + 16 * blocks + 8]


def plan_kernel(parts, lengths, spot, info, *refs):
    tables, lists, ends = refs[:len(parts)], refs[len(parts):-1], refs[-1]
    x, y, core = spot[0], spot[1], spot[2]

    def within(x, y):
        return (x // 2) * 2048 + y * 512 + (x % 2) * 256

    place = within(x, y)
    info[0] = place
    info[1] = core

    def add_up(k, end):
        end = end + lengths[k] * BLOCK
        ends[k + 1] = end
        return end

    ends[0] = jnp.int32(0)
    lax.fori_loop(0, 16, add_up, jnp.int32(0))

    def query_plane(z, k):
        at = 4 + z * 6
        for b in range(4):
            token = z * PLANE + place + b * BLOCK
            k = lax.while_loop(lambda k: ends[k + 1] <= token, lambda k: k + 1, k)
            start = ends[k]
            info[at + jnp.where(core == b // 2, 0, 2) + b % 2] = start
            if b == 0:
                info[at + 4] = start
            if b == 3:
                info[at + 5] = start
        return k

    lax.fori_loop(0, 8, query_plane, jnp.int32(0))

    for (far, blocks), table, out in zip(parts, tables, lists):
        wide = blocks // 8
        *kinds, plain_b, mixed_b, _ = layout(blocks)
        for half in range(2):
            for n in range(wide):
                d, e = far[n // 4], SHIFTS[n % 4]
                dx, dy = (e, d) if half == 0 else (d, e)
                first = within((x + dx + 4) % 4, (y + dy + 4) % 4) + core * TILE
                for p in range(4):
                    table[half * 4 * wide + n * 4 + p] = first + (half * 4 + p) * PLANE

        def plane(z, counts, table=table, out=out, wide=wide, kinds=kinds, plain_b=plain_b, mixed_b=mixed_b):
            plain, mixed, *counts = counts
            begin = z * PLANE + place
            low = info[4 + z * 6 + 4]

            def key_plane(zk, found):
                p, m = found
                b = (zk // 4) * (4 * wide) + zk % 4
                for n in range(wide):
                    base = table[b + n * 4]
                    need = (base + (TILE - 1) >= low) & (base <= begin + 255)
                    clear = (base + (TILE - 1) < begin) & (base >= low)
                    out[p] = b + n * 4
                    out[m] = b + n * 4
                    p, m = p + jnp.where(need & clear, 1, 0), m + jnp.where(need & ~clear, 1, 0)
                return p, m

            p, m = lax.fori_loop(low // PLANE, z + 1, key_plane, (plain_b + plain, mixed_b + mixed))
            plain_at, mixed_at = plain_b + plain, mixed_b + mixed
            left, more = p - plain_at, m - mixed_at
            for kind, (size, masked) in enumerate(UNITS):
                at, count = (mixed_at, more) if masked else (plain_at, left)
                n = count // size

                def name(i, carry, kind=kind, size=size, at=at, first=counts[kind]):
                    out[kinds[kind] + first + i] = (at + i * size) * 8 + z
                    return carry

                lax.fori_loop(0, n, name, 0)
                counts[kind] = counts[kind] + n
                if masked:
                    mixed_at, more = at + n * size, count - n * size
                else:
                    plain_at, left = at + n * size, count - n * size
            return (p - plain_b, m - mixed_b, *counts)

        none = (jnp.int32(0),) * (2 + len(UNITS))
        counts = lax.fori_loop(0, 8, plane, none)[2:]
        for kind, count in enumerate(counts):
            out[kind] = count


def plan(lengths):
    spot = jnp.stack([lax.axis_index("xh") * 2 + lax.axis_index("xl"), lax.axis_index("y"), lax.axis_index("c")])
    smem = pl.BlockSpec(memory_space=pltpu.SMEM)
    parts = [((0,), 32), ((-1, 1), 64), ((2,), 32)]
    sizes = [52] + [b for _, b in parts] + [layout(b)[-1] for _, b in parts]
    info, *rest = pl.pallas_call(
        functools.partial(plan_kernel, parts),
        out_shape=[jax.ShapeDtypeStruct((n,), jnp.int32) for n in sizes],
        in_specs=[smem] * 2,
        out_specs=[smem] * len(sizes),
        scratch_shapes=[pltpu.SMEM((17,), jnp.int32)],
    )(lengths, spot.astype(jnp.int32))
    return info, rest[:3], rest[3:]


def prepare_kernel(keys, values, out):
    for head in range(2):
        lanes = slice(head * HD, head * HD + HD)
        k = keys[:, lanes]
        vt = values[:, lanes].astype(jnp.float32).T.astype(jnp.bfloat16)
        for z in range(head, 8, 2):
            out[z, :, :HD] = k
            out[z, :, HD:] = vt


def prepare(keys, values):
    whole = pl.BlockSpec(memory_space=pltpu.VMEM)
    return pl.pallas_call(
        prepare_kernel,
        out_shape=jax.ShapeDtypeStruct((8, TILE, 2 * HD), jnp.bfloat16),
        in_specs=[whole] * 2,
        out_specs=whole,
    )(keys, values)


def pack_kernel(count, *refs):
    for half in range(2):
        at = 0
        for source in refs[half * count:(half + 1) * count]:
            refs[2 * count + half][at:at + source.shape[0]] = source[...]
            at += source.shape[0]


def pack(*halves):
    count = len(halves[0])
    whole = pl.BlockSpec(memory_space=pltpu.VMEM)
    out = [jax.ShapeDtypeStruct((sum(p.shape[0] for p in half),) + half[0].shape[1:], half[0].dtype) for half in halves]
    return pl.pallas_call(
        functools.partial(pack_kernel, count),
        out_shape=out,
        in_specs=[whole] * (2 * count),
        out_specs=[whole] * 2,
        compiler_params=pltpu.CompilerParams(vmem_limit_bytes=12 * 2**20),
    )(*halves[0], *halves[1])


def attend_kernel(blocks, first, last, moves, *refs):
    info, table, lists = refs[:3]
    rest = list(refs[3:])
    if first:
        q_own, q_other = rest[:2]
        del rest[:2]
    else:
        state = rest[:4]
        del rest[:4]
    sources = rest[:len(moves)]
    del rest[:len(moves)]
    if first:
        qq = rest.pop(0)
    else:
        qq = state[0]
    if last:
        o_own, o_other, lse_own, lse_other = rest[:4]
        del rest[:4]
    acc, peak, total, kv, score, weight, top, fade, off, sems = rest
    kinds = layout(blocks)

    copies = [pltpu.make_async_copy(src, kv.at[pl.ds(at, size)], sems.at[i])
              for i, (src, (at, size)) in enumerate(zip(sources, moves))]
    for copy in copies:
        copy.start()
    place = info[0]
    core = info[1]
    if first:
        for half, ref in enumerate((q_own, q_other)):
            for head in range(2):
                full = ref[:, head].astype(jnp.float32) * LOG2E_SCALE
                high = full.astype(jnp.bfloat16)
                lanes = slice(head * 256 + half * 128, head * 256 + half * 128 + 128)
                qq[:, :HD, lanes] = high
                qq[:, HD:, lanes] = (full - high.astype(jnp.float32)).astype(jnp.bfloat16)
        acc[...] = jnp.zeros_like(acc)
        total[...] = jnp.zeros_like(total)
        peak[...] = jnp.full_like(peak, FLOOR)
    else:
        for ref, old in zip((acc, peak, total), state[1:]):
            ref[...] = old[...]
    for copy in copies:
        copy.wait()

    def bounds(z):
        lane = lax.broadcasted_iota(jnp.int32, (1, 512), 1) % 256
        b = lane // 64
        at = 4 + z * 6
        start = jnp.where(b == 0, info[at], jnp.where(b == 1, info[at + 1],
                          jnp.where(b == 2, info[at + 2], info[at + 3])))
        part = jnp.where(lane < 128, core, 1 - core) * 128
        return start, z * PLANE + place + part + lane % 128

    for z in range(8):
        late = bounds(z)[0] > z * PLANE + place
        off[z] = jnp.broadcast_to(jnp.where(late, NEVER, 0.0), (8, 512))

    def run(kind):
        wide, masked = UNITS[kind]
        keys = wide * TILE
        count = lists[kind]

        def plane_of(i):
            return lists[kinds[kind] + i] % 8

        def block(i, g):
            return lists[lists[kinds[kind] + i] // 8 + g]

        def scores_of(i):
            z = plane_of(i)
            k = jnp.concatenate([kv[block(i, g), :, :HD] for g in range(wide)], axis=0)
            s = jnp.dot(jnp.concatenate([k, k], axis=1), qq[z], preferred_element_type=jnp.float32)
            if masked:
                start, stop = bounds(z)
                row = lax.broadcasted_iota(jnp.int32, (TILE, 512), 0)
                parts = []
                for g in range(wide):
                    base = table[block(i, g)]
                    keep = (row >= start - base) & (row <= stop - base)
                    parts.append(jnp.where(keep, s[g * TILE:(g + 1) * TILE], MASKED))
                s = jnp.concatenate(parts, axis=0)
            score[:keys, :] = s
            top[...] = jnp.max(s.reshape(keys // 8, 8, 512), axis=0)

        def weigh(i):
            z = plane_of(i)
            old = peak[z]
            most = jnp.max(top[...], axis=0, keepdims=True)
            new = jnp.maximum(old, most if masked else most - off[z])
            factor = jnp.exp2(old - new)
            fade[...] = factor
            peak[z] = new
            if not masked:
                new = new + off[z]
            sums = total[z] * factor
            for u in range(keys // 16):
                rows = slice(u * 16, u * 16 + 16)
                p = jnp.exp2(score[rows, :].reshape(2, 8, 512) - new)
                sums = sums + (p[0] + p[1])
                weight[rows, :] = p.reshape(16, 512).astype(jnp.bfloat16)
            total[z] = sums

        def collect(i):
            z = plane_of(i)
            v = jnp.concatenate([kv[block(i, g), :, HD:] for g in range(wide)], axis=1)
            pv = jnp.dot(v, weight[:keys, :], preferred_element_type=jnp.float32)
            acc[z] = (acc[z].reshape(16, 8, 512) * fade[...] + pv.reshape(16, 8, 512)).reshape(HD, 512)

        @pl.when(count > 0)
        def _():
            scores_of(0)
            weight[:keys, :] = jnp.zeros((keys, 512), jnp.bfloat16)
            fade[...] = jnp.ones_like(fade)

            def body(i, carry):
                collect(jnp.maximum(i - 1, 0))
                weigh(i)
                scores_of(jnp.minimum(i + 1, count - 1))
                return carry

            lax.fori_loop(0, count, body, 0)
            collect(count - 1)

    for kind in range(len(UNITS)):
        run(kind)
    if last:
        for z in range(8):
            l = jnp.sum(total[z], axis=0, keepdims=True)
            o = acc[z] / jnp.where(l > 0, l, 1.0)
            lse = jnp.where(l > 0, peak[z, :1] + jnp.log2(jnp.where(l > 0, l, 1.0)), FLOOR)
            for head in range(2):
                for half, (o_ref, lse_ref) in enumerate(((o_own, lse_own), (o_other, lse_other))):
                    lanes = slice(head * 256 + half * 128, head * 256 + half * 128 + 128)
                    o_ref[z, head] = o[:, lanes].astype(o_ref.dtype)
                    lse_ref[z, head] = jnp.broadcast_to(lse[:, lanes], (8, TILE))


def attend(info, table, lists, queries, state, sources, last, cost):
    vmem = pltpu.VMEM
    f32, bf16 = jnp.float32, jnp.bfloat16
    first = state is None
    sizes = [s.shape[0] for s in sources]
    blocks = sum(sizes)
    moves = [(sum(sizes[:i]), size) for i, size in enumerate(sizes)]
    keys = WIDEST * TILE
    whole = pl.BlockSpec(memory_space=vmem)
    smem = pl.BlockSpec(memory_space=pltpu.SMEM)
    held = [jax.ShapeDtypeStruct((8, 2 * HD, 512), bf16), jax.ShapeDtypeStruct((8, HD, 512), f32),
            jax.ShapeDtypeStruct((8, 8, 512), f32), jax.ShapeDtypeStruct((8, 8, 512), f32)]
    o = jax.ShapeDtypeStruct((8, 2, HD, TILE), bf16)
    lse = jax.ShapeDtypeStruct((8, 2, 8, TILE), f32)
    before = list(queries) if first else list(state)
    return pl.pallas_call(
        functools.partial(attend_kernel, blocks, first, last, moves),
        out_shape=[o, o, lse, lse] if last else held if first else held[1:],
        in_specs=[smem, smem, smem] + [whole] * len(before)
        + [pl.BlockSpec(memory_space=pl.ANY)] * len(sources),
        out_specs=[whole] * (4 if first or last else 3),
        scratch_shapes=[vmem(h.shape, h.dtype) for h in held[1:] if last] + [
            vmem((blocks, TILE, 2 * HD), bf16),
            vmem((keys, 512), f32),
            vmem((keys, 512), bf16),
            vmem((8, 512), f32),
            vmem((8, 512), f32),
            vmem((8, 8, 512), f32),
            pltpu.SemaphoreType.DMA((len(moves),)),
        ],
        compiler_params=pltpu.CompilerParams(vmem_limit_bytes=30 * 2**20),
        cost_estimate=pl.CostEstimate(flops=int(cost * 1e9), bytes_accessed=8 * 2**20, transcendentals=0),
    )(info, table, lists, *before, *sources)


def ring(n, d):
    return [(i, (i + d) % n) for i in range(n)]


def shards(queries, keys, values, lengths):
    swap = [(0, 1), (1, 0)]
    kv_send = prepare(keys, values)
    kv_z = lax.all_to_all(kv_send, "z", split_axis=0, concat_axis=0, tiled=True)
    qt = queries.reshape(TILE, 2, 4, 2, HD).transpose(2, 1, 3, 4, 0).reshape(8, 2, HD, TILE)
    planned = plan(lengths)
    qt, kv_z, planned = lax.optimization_barrier((qt, kv_z, planned))
    info, tables, lists = planned
    q_own = lax.all_to_all(qt, "z", split_axis=0, concat_axis=0, tiled=True)
    q_other = lax.ppermute(q_own, "c", swap)

    def shift(value, axis, d):
        return lax.ppermute(value, axis, ring(4, d))

    xs, ys = ("xh", "xl"), "y"
    first, second = kv_z[:4], kv_z[4:]
    near_a = [first] + [shift(first, xs, -d) for d in SHIFTS[1:]]
    near_b = [second] + [shift(second, ys, -d) for d in SHIFTS[1:]]
    part_a, part_b = pack(near_a, near_b)
    a_up, a_down = shift(part_a, ys, 1), shift(part_a, ys, -1)
    b_up, b_down = shift(part_b, xs, 1), shift(part_b, xs, -1)
    qq, *state = attend(info, tables[0], lists[0], (q_own, q_other), None, [part_a, part_b], False, 4)
    a_up, b_down, qq, state = lax.optimization_barrier((a_up, b_down, qq, state))
    a_far, b_far = shift(a_up, ys, 1), shift(b_down, xs, -1)
    state = attend(info, tables[1], lists[1], None, [qq, *state], [a_up, a_down, b_up, b_down], False, 8)
    o_own, o_other, lse_own, lse_other = attend(
        info, tables[2], lists[2], None, [qq, *state], [a_far, b_far], True, 4)

    o_got = lax.ppermute(o_other, "c", swap)
    lse_got = lax.ppermute(lse_other, "c", swap)
    a, b = lse_own[:, :, :1], lse_got[:, :, :1]
    most = jnp.maximum(a, b)
    wa, wb = jnp.exp2(a - most), jnp.exp2(b - most)
    o = (o_own.astype(jnp.float32) * wa + o_got.astype(jnp.float32) * wb) / (wa + wb)
    back = lax.all_to_all(o.astype(jnp.bfloat16), "z", split_axis=0, concat_axis=0, tiled=True)
    return back.reshape(4, 2, 2, HD, TILE).transpose(4, 1, 0, 2, 3).reshape(TILE, 16 * HD)


def solution(mesh):
    fine = Mesh(mesh.devices.reshape(SIZES), AXES)
    spec = P(AXES, None)
    return jax.shard_map(
        shards, mesh=fine, in_specs=(spec, spec, spec, P()), out_specs=spec, check_vma=False
    )
```

profile of v0, /device:TPU:6, one launch (start us, length us, event | category | flops | bytes accessed | tf_op | source)
XLA Modules:
  0.0 139.3 jit_solution(10431111495913111001)
XLA Ops:
  0.0 1.8 %shard_map.46 = bf16[8,128,256]{2,1,0:T(8,128)(2,1)} custom-call(bf16[128,256]{1,0:T(8,128)(2,1)} %keys.1, bf16[128,256]{1,0:T(8,128)(2,1)} %values.1), custom_call_target="tpu_custom_call" | custom-call | tf_op jit(solution)/shard_map/pallas_call | solution.py:148
  1.8 8.5 %all-to-all-start = ((bf16[8,128,256]{2,1,0:T(8,128)(2,1)}), bf16[8,128,256]{2,1,0:T(8,128)(2,1)S(1)}, u32[]{:S(2)}, u32[]{:S(2)}) async-start(bf16[8,128,256]{2,1,0:T(8,128)(2,1)} %shard_map.46), calls=%async_computation | async-start | bytes 1048576 | tf_op jit(solution)/shard_map/all_to_all | solution.py:356
  10.3 1.4 %reshape.12 = bf16[128,2,4,2,128]{4,3,2,1,0:T(2,128)(2,1)S(1)} reshape(bf16[128,2048]{1,0:T(8,128)(2,1)} %param.4) | data formatting | bytes 1048576 | tf_op jit(solution)/shard_map/reshape | solution.py:357
  11.7 1.3 copy.5
  12.9 0.6 pad_add_fusion.spot
  13.5 6.9 %shard_map.47 = (s32[52]{0:T(128)}, s32[32]{0:T(128)}, s32[64]{0:T(128)}, s32[32]{0:T(128)}, s32[607]{0:T(1024)}, /*index=5*/s32[1151]{0:T(1024)}, s32[607]{0:T(1024)}) custom-call(s32[16]{0:T(128)} %lengths.1, s32[3]{0:T(128)} %pad_add_fusion.spot), custom_call_target="tpu_custom_call" | custom-call | tf_op jit(solution)/shard_map/pallas_call | solution.py:126
  20.4 7.3 %all-to-all-done = bf16[8,128,256]{2,1,0:T(8,128)(2,1)S(1)} async-done(((bf16[8,128,256]{2,1,0:T(8,128)(2,1)}), bf16[8,128,256]{2,1,0:T(8,128)(2,1)S(1)}, u32[]{:S(2)}, u32[]{:S(2)}) %all-to-all-start) | async-done | bytes 524320 | tf_op jit(solution)/shard_map/all_to_all | solution.py:356
  27.8 3.6 %all-to-all-start.1 = ((bf16[8,2,128,128]{3,2,1,0:T(8,128)(2,1)}), bf16[8,2,128,128]{3,2,1,0:T(8,128)(2,1)S(1)}, u32[]{:S(2)}, u32[]{:S(2)}) async-start(bf16[8,2,128,128]{3,2,1,0:T(8,128)(2,1)} %bitcast.1), calls=%async_computation.1 | async-start | bytes 1048576 | tf_op jit(solution)/shard_map/all_to_all | solution.py:361
  32.0 1.5 %collective-permute-start.1 = (bf16[4,128,256]{2,1,0:T(8,128)(2,1)S(1)}, bf16[4,128,256]{2,1,0:T(8,128)(2,1)S(1)}, u32[]{:S(2)}, u32[]{:S(2)}) collective-permute-start(bf16[4,128,256]{2,1,0:T(8,128)(2,1)S(1)} %get-tuple-element.79.refs_0_), channel_id=1, source_target_pairs={{0,18},{2,0},{16,2},{18,16},{1,19},{3,1},{17,3},{19,17},{4,22},{6,... | collective-permute-start | bytes 786440 | tf_op jit(solution)/shard_map/ppermute | solution.py:365
  33.5 1.4 %collective-permute-start.2 = (bf16[4,128,256]{2,1,0:T(8,128)(2,1)S(1)}, bf16[4,128,256]{2,1,0:T(8,128)(2,1)S(1)}, u32[]{:S(2)}, u32[]{:S(2)}) collective-permute-start(bf16[4,128,256]{2,1,0:T(8,128)(2,1)S(1)} %get-tuple-element.79.refs_0_), channel_id=1, source_target_pairs={{0,16},{2,18},{16,0},{18,2},{1,17},{3,19},{17,1},{19,3},{4,20},{6,... | collective-permute-start | bytes 786440 | tf_op jit(solution)/shard_map/ppermute | solution.py:365
  34.9 1.6 %collective-permute-start.3 = (bf16[4,128,256]{2,1,0:T(8,128)(2,1)S(1)}, bf16[4,128,256]{2,1,0:T(8,128)(2,1)S(1)}, u32[]{:S(2)}, u32[]{:S(2)}) collective-permute-start(bf16[4,128,256]{2,1,0:T(8,128)(2,1)S(1)} %get-tuple-element.78.refs_4_), channel_id=1, source_target_pairs={{0,4},{4,8},{8,12},{12,0},{1,5},{5,9},{9,13},{13,1},{2,6},{6,10},{... | collective-permute-start | bytes 786440 | tf_op jit(solution)/shard_map/ppermute | solution.py:365
  36.5 1.7 %collective-permute-start.4 = (bf16[4,128,256]{2,1,0:T(8,128)(2,1)S(1)}, bf16[4,128,256]{2,1,0:T(8,128)(2,1)S(1)}, u32[]{:S(2)}, u32[]{:S(2)}) collective-permute-start(bf16[4,128,256]{2,1,0:T(8,128)(2,1)S(1)} %get-tuple-element.78.refs_4_), channel_id=1, source_target_pairs={{0,12},{4,0},{8,4},{12,8},{1,13},{5,1},{9,5},{13,9},{2,14},{6,2},{... | collective-permute-start | bytes 786440 | tf_op jit(solution)/shard_map/ppermute | solution.py:365
  38.2 2.5 %collective-permute-done.refs_1_ = bf16[4,128,256]{2,1,0:T(8,128)(2,1)S(1)} collective-permute-done((bf16[4,128,256]{2,1,0:T(8,128)(2,1)S(1)}, bf16[4,128,256]{2,1,0:T(8,128)(2,1)S(1)}, u32[]{:S(2)}, u32[]{:S(2)}) %collective-permute-start) | collective-permute-done | bytes 262176 | tf_op jit(solution)/shard_map/ppermute | solution.py:365
  40.7 3.2 %collective-permute-start.5 = (bf16[4,128,256]{2,1,0:T(8,128)(2,1)S(1)}, bf16[4,128,256]{2,1,0:T(8,128)(2,1)S(1)}, u32[]{:S(2)}, u32[]{:S(2)}) collective-permute-start(bf16[4,128,256]{2,1,0:T(8,128)(2,1)S(1)} %get-tuple-element.78.refs_4_), channel_id=1, source_target_pairs={{0,8},{4,12},{8,0},{12,4},{1,9},{5,13},{9,1},{13,5},{2,10},{6,14},... | collective-permute-start | bytes 786440 | tf_op jit(solution)/shard_map/ppermute | solution.py:365
  43.9 2.9 %collective-permute-done.1.refs_2_ = bf16[4,128,256]{2,1,0:T(8,128)(2,1)S(1)} collective-permute-done((bf16[4,128,256]{2,1,0:T(8,128)(2,1)S(1)}, bf16[4,128,256]{2,1,0:T(8,128)(2,1)S(1)}, u32[]{:S(2)}, u32[]{:S(2)}) %collective-permute-start.1) | collective-permute-done | bytes 262176 | tf_op jit(solution)/shard_map/ppermute | solution.py:365
  46.8 3.6 %collective-permute-done.5.refs_7_ = bf16[4,128,256]{2,1,0:T(8,128)(2,1)S(1)} collective-permute-done((bf16[4,128,256]{2,1,0:T(8,128)(2,1)S(1)}, bf16[4,128,256]{2,1,0:T(8,128)(2,1)S(1)}, u32[]{:S(2)}, u32[]{:S(2)}) %collective-permute-start.5) | collective-permute-done | bytes 262176 | tf_op jit(solution)/shard_map/ppermute | solution.py:365
  50.4 1.5 %shard_map.48 = (bf16[16,128,256]{2,1,0:T(8,128)(2,1)}, bf16[16,128,256]{2,1,0:T(8,128)(2,1)}) custom-call(bf16[4,128,256]{2,1,0:T(8,128)(2,1)S(1)} %get-tuple-element.79.refs_0_, bf16[4,128,256]{2,1,0:T(8,128)(2,1)S(1)} %collective-permute-done.refs_1_, bf16[4,128,256]{2,1,0:T(8,128)(2,1)S(1)} %collective-permute-done.1.refs_2_, ...), custom_call_target="tpu_custom_call" | custom-call | tf_op jit(solution)/shard_map/pallas_call | solution.py:168
  51.9 1.1 collective-permute-start.6
  53.0 1.1 collective-permute-start.7
  54.2 2.1 %collective-permute-start.9 = (bf16[16,128,256]{2,1,0:T(8,128)(2,1)}, bf16[16,128,256]{2,1,0:T(8,128)(2,1)S(1)}, u32[]{:S(2)}, u32[]{:S(2)}) collective-permute-start(bf16[16,128,256]{2,1,0:T(8,128)(2,1)} %get-tuple-element.51.refs_5_), channel_id=1, source_target_pairs={{0,12},{4,0},{8,4},{12,8},{1,13},{5,1},{9,5},{13,9},{2,14},{6,2},{... | collective-permute-start | bytes 3145736 | tf_op jit(solution)/shard_map/ppermute | solution.py:365
  56.3 2.1 %collective-permute-start.10 = (bf16[16,128,256]{2,1,0:T(8,128)(2,1)}, bf16[16,128,256]{2,1,0:T(8,128)(2,1)S(1)}, u32[]{:S(2)}, u32[]{:S(2)}) collective-permute-start(bf16[16,128,256]{2,1,0:T(8,128)(2,1)} %get-tuple-element.52.refs_6_), channel_id=1, source_target_pairs={{0,2},{2,16},{16,18},{18,0},{1,3},{3,17},{17,19},{19,1},{4,6},{6,2... | collective-permute-start | bytes 3145736 | tf_op jit(solution)/shard_map/ppermute | solution.py:365
  58.4 12.4 %shard_map.49 = (bf16[8,256,512]{2,1,0:T(8,128)(2,1)S(1)}, f32[8,128,512]{2,1,0:T(8,128)S(1)}, f32[8,8,512]{2,1,0:T(8,128)S(1)}, f32[8,8,512]{2,1,0:T(8,128)S(1)}) custom-call(s32[52]{0:T(128)S(1)} %copy-done.3, s32[32]{0:T(128)S(1)} %copy-done.6, s32[607]{0:T(1024)S(1)} %copy-done.2, bf16[8,2,128,128]{3,2,1,0:T(8,128)(2,1)S(1)} %all-to-all-done.1.refs_3_, ...), custom_call_target="tpu_custom_call" | custom-call | flops 4000000000 | bytes 8388608 | tf_op jit(solution)/shard_map/pallas_call | solution.py:329
  70.8 6.0 %collective-permute-done.6.refs_7_ = bf16[16,128,256]{2,1,0:T(8,128)(2,1)S(1)} collective-permute-done((bf16[16,128,256]{2,1,0:T(8,128)(2,1)}, bf16[16,128,256]{2,1,0:T(8,128)(2,1)S(1)}, u32[]{:S(2)}, u32[]{:S(2)}) %collective-permute-start.6) | collective-permute-done | bytes 1048608 | tf_op jit(solution)/shard_map/ppermute | solution.py:365
  76.8 1.1 collective-permute-done.7.refs_10_
  78.3 1.7 %collective-permute-done.9.refs_8_ = bf16[16,128,256]{2,1,0:T(8,128)(2,1)S(1)} collective-permute-done((bf16[16,128,256]{2,1,0:T(8,128)(2,1)}, bf16[16,128,256]{2,1,0:T(8,128)(2,1)S(1)}, u32[]{:S(2)}, u32[]{:S(2)}) %collective-permute-start.9) | collective-permute-done | bytes 1048608 | tf_op jit(solution)/shard_map/ppermute | solution.py:365
  80.0 1.8 %collective-permute-done.10.refs_9_ = bf16[16,128,256]{2,1,0:T(8,128)(2,1)S(1)} collective-permute-done((bf16[16,128,256]{2,1,0:T(8,128)(2,1)}, bf16[16,128,256]{2,1,0:T(8,128)(2,1)S(1)}, u32[]{:S(2)}, u32[]{:S(2)}) %collective-permute-start.10) | collective-permute-done | bytes 1048608 | tf_op jit(solution)/shard_map/ppermute | solution.py:365
  81.8 16.9 %shard_map.50 = (f32[8,128,512]{2,1,0:T(8,128)S(1)}, f32[8,8,512]{2,1,0:T(8,128)S(1)}, f32[8,8,512]{2,1,0:T(8,128)S(1)}) custom-call(s32[52]{0:T(128)S(1)} %copy-done.3, s32[64]{0:T(128)S(1)} %copy-done.5, s32[1151]{0:T(1024)S(1)} %copy-done, bf16[8,256,512]{2,1,0:T(8,128)(2,1)S(1)} %get-tuple-element.60.refs_3_, ...), custom_call_target="tpu_custom_call" | custom-call | flops 8000000000 | bytes 8388608 | tf_op jit(solution)/shard_map/pallas_call | solution.py:329
  98.7 2.9 %collective-permute-done.11.refs_7_ = bf16[16,128,256]{2,1,0:T(8,128)(2,1)S(1)} collective-permute-done((bf16[16,128,256]{2,1,0:T(8,128)(2,1)S(1)}, bf16[16,128,256]{2,1,0:T(8,128)(2,1)S(1)}, u32[]{:S(2)}, u32[]{:S(2)}) %collective-permute-start.11) | collective-permute-done | bytes 1048608 | tf_op jit(solution)/shard_map/ppermute | solution.py:365
  101.8 9.7 %shard_map.51 = (bf16[8,2,128,128]{3,2,1,0:T(8,128)(2,1)S(1)}, bf16[8,2,128,128]{3,2,1,0:T(8,128)(2,1)S(1)}, f32[8,2,8,128]{3,2,1,0:T(8,128)S(1)}, f32[8,2,8,128]{3,2,1,0:T(8,128)S(1)}) custom-call(s32[52]{0:T(128)S(1)} %copy-done.3, s32[32]{0:T(128)S(1)} %copy-done.4, s32[607]{0:T(1024)S(1)} %copy-done.1, ...), custom_call_target="tpu_custom_call" | custom-call | flops 4000000000 | bytes 8388608 | tf_op jit(solution)/shard_map/pallas_call | solution.py:329
  112.2 1.5 %collective-permute-done.13 = f32[8,2,8,128]{3,2,1,0:T(8,128)S(1)} collective-permute-done((f32[8,2,8,128]{3,2,1,0:T(8,128)S(1)}, f32[8,2,8,128]{3,2,1,0:T(8,128)S(1)}, u32[]{:S(2)}, u32[]{:S(2)}) %collective-permute-start.13) | collective-permute-done | bytes 65568 | tf_op jit(solution)/shard_map/ppermute | solution.py:382
  114.0 23.7 %all_to_all.15 = bf16[8,2,128,128]{3,2,1,0:T(8,128)(2,1)S(1)} all-to-all(bf16[8,2,128,128]{3,2,1,0:T(8,128)(2,1)S(1)} %divide_convert_fusion), channel_id=1, replica_groups=mesh['z'=8,'xh'=2,'y'=4,'xl'=2,'c'=2] {'z'}, dimensions={0} | all-to-all | bytes 1048576 | tf_op jit(solution)/shard_map/all_to_all | solution.py:387
  138.1 1.2 reshape.15
  (31 shorter events, 2.6 us)
Async XLA Ops:
  1.8 26.0 %all-to-all-start = ((bf16[8,128,256]{2,1,0:T(8,128)(2,1)}), bf16[8,128,256]{2,1,0:T(8,128)(2,1)S(1)}, u32[]{:S(2)}, u32[]{:S(2)}) async-start(bf16[8,128,256]{2,1,0:T(8,128)(2,1)} %shard_map.46), calls=%async_computation | async-start | bytes 1048576 | tf_op jit(solution)/shard_map/all_to_all | solution.py:356
  27.7 30.6 %copy-start.2 = (s32[607]{0:T(1024)S(1)}, s32[607]{0:T(1024)}, u32[]{:S(2)}) copy-start(s32[607]{0:T(1024)} %get-tuple-element.54.refs_2_) | copy-start | bytes 7288
  27.7 30.6 %copy-start.3 = (s32[52]{0:T(128)S(1)}, s32[52]{0:T(128)}, u32[]{:S(2)}) copy-start(s32[52]{0:T(128)} %get-tuple-element.47.refs_0_) | copy-start | bytes 628
  27.8 30.6 %copy-start.6 = (s32[32]{0:T(128)S(1)}, s32[32]{0:T(128)}, u32[]{:S(2)}) copy-start(s32[32]{0:T(128)} %get-tuple-element.53.refs_1_) | copy-start | bytes 388
  27.8 26.4 %all-to-all-start.1 = ((bf16[8,2,128,128]{3,2,1,0:T(8,128)(2,1)}), bf16[8,2,128,128]{3,2,1,0:T(8,128)(2,1)S(1)}, u32[]{:S(2)}, u32[]{:S(2)}) async-start(bf16[8,2,128,128]{3,2,1,0:T(8,128)(2,1)} %bitcast.1), calls=%async_computation.1 | async-start | bytes 1048576 | tf_op jit(solution)/shard_map/all_to_all | solution.py:361
  31.4 9.2 %collective-permute-start = (bf16[4,128,256]{2,1,0:T(8,128)(2,1)S(1)}, bf16[4,128,256]{2,1,0:T(8,128)(2,1)S(1)}, u32[]{:S(2)}, u32[]{:S(2)}) collective-permute-start(bf16[4,128,256]{2,1,0:T(8,128)(2,1)S(1)} %get-tuple-element.79.refs_0_), channel_id=1, source_target_pairs={{0,2},{2,16},{16,18},{18,0},{1,3},{3,17},{17,19},{19,1},{4,6},{6,2... | collective-permute-start | bytes 786440 | tf_op jit(solution)/shard_map/ppermute | solution.py:365
  32.0 14.8 %collective-permute-start.1 = (bf16[4,128,256]{2,1,0:T(8,128)(2,1)S(1)}, bf16[4,128,256]{2,1,0:T(8,128)(2,1)S(1)}, u32[]{:S(2)}, u32[]{:S(2)}) collective-permute-start(bf16[4,128,256]{2,1,0:T(8,128)(2,1)S(1)} %get-tuple-element.79.refs_0_), channel_id=1, source_target_pairs={{0,18},{2,0},{16,2},{18,16},{1,19},{3,1},{17,3},{19,17},{4,22},{6,... | collective-permute-start | bytes 786440 | tf_op jit(solution)/shard_map/ppermute | solution.py:365
  33.5 13.2 %collective-permute-start.2 = (bf16[4,128,256]{2,1,0:T(8,128)(2,1)S(1)}, bf16[4,128,256]{2,1,0:T(8,128)(2,1)S(1)}, u32[]{:S(2)}, u32[]{:S(2)}) collective-permute-start(bf16[4,128,256]{2,1,0:T(8,128)(2,1)S(1)} %get-tuple-element.79.refs_0_), channel_id=1, source_target_pairs={{0,16},{2,18},{16,0},{18,2},{1,17},{3,19},{17,1},{19,3},{4,20},{6,... | collective-permute-start | bytes 786440 | tf_op jit(solution)/shard_map/ppermute | solution.py:365
  34.9 11.8 %collective-permute-start.3 = (bf16[4,128,256]{2,1,0:T(8,128)(2,1)S(1)}, bf16[4,128,256]{2,1,0:T(8,128)(2,1)S(1)}, u32[]{:S(2)}, u32[]{:S(2)}) collective-permute-start(bf16[4,128,256]{2,1,0:T(8,128)(2,1)S(1)} %get-tuple-element.78.refs_4_), channel_id=1, source_target_pairs={{0,4},{4,8},{8,12},{12,0},{1,5},{5,9},{9,13},{13,1},{2,6},{6,10},{... | collective-permute-start | bytes 786440 | tf_op jit(solution)/shard_map/ppermute | solution.py:365
  36.5 10.3 %collective-permute-start.4 = (bf16[4,128,256]{2,1,0:T(8,128)(2,1)S(1)}, bf16[4,128,256]{2,1,0:T(8,128)(2,1)S(1)}, u32[]{:S(2)}, u32[]{:S(2)}) collective-permute-start(bf16[4,128,256]{2,1,0:T(8,128)(2,1)S(1)} %get-tuple-element.78.refs_4_), channel_id=1, source_target_pairs={{0,12},{4,0},{8,4},{12,8},{1,13},{5,1},{9,5},{13,9},{2,14},{6,2},{... | collective-permute-start | bytes 786440 | tf_op jit(solution)/shard_map/ppermute | solution.py:365
  40.7 9.7 %collective-permute-start.5 = (bf16[4,128,256]{2,1,0:T(8,128)(2,1)S(1)}, bf16[4,128,256]{2,1,0:T(8,128)(2,1)S(1)}, u32[]{:S(2)}, u32[]{:S(2)}) collective-permute-start(bf16[4,128,256]{2,1,0:T(8,128)(2,1)S(1)} %get-tuple-element.78.refs_4_), channel_id=1, source_target_pairs={{0,8},{4,12},{8,0},{12,4},{1,9},{5,13},{9,1},{13,5},{2,10},{6,14},... | collective-permute-start | bytes 786440 | tf_op jit(solution)/shard_map/ppermute | solution.py:365
  51.9 24.9 %collective-permute-start.6 = (bf16[16,128,256]{2,1,0:T(8,128)(2,1)}, bf16[16,128,256]{2,1,0:T(8,128)(2,1)S(1)}, u32[]{:S(2)}, u32[]{:S(2)}) collective-permute-start(bf16[16,128,256]{2,1,0:T(8,128)(2,1)} %get-tuple-element.51.refs_5_), channel_id=1, source_target_pairs={{0,4},{4,8},{8,12},{12,0},{1,5},{5,9},{9,13},{13,1},{2,6},{6,10},{... | collective-permute-start | bytes 3145736 | tf_op jit(solution)/shard_map/ppermute | solution.py:365
  53.0 28.8 %copy-start = (s32[1151]{0:T(1024)S(1)}, s32[1151]{0:T(1024)}, u32[]{:S(2)}) copy-start(s32[1151]{0:T(1024)} %get-tuple-element.62.refs_2_) | copy-start | bytes 13816
  53.0 28.8 %copy-start.5 = (s32[64]{0:T(128)S(1)}, s32[64]{0:T(128)}, u32[]{:S(2)}) copy-start(s32[64]{0:T(128)} %get-tuple-element.61.refs_1_) | copy-start | bytes 772
  53.0 24.9 %collective-permute-start.7 = (bf16[16,128,256]{2,1,0:T(8,128)(2,1)}, bf16[16,128,256]{2,1,0:T(8,128)(2,1)S(1)}, u32[]{:S(2)}, u32[]{:S(2)}) collective-permute-start(bf16[16,128,256]{2,1,0:T(8,128)(2,1)} %get-tuple-element.52.refs_6_), channel_id=1, source_target_pairs={{0,18},{2,0},{16,2},{18,16},{1,19},{3,1},{17,3},{19,17},{4,22},{6,... | collective-permute-start | bytes 3145736 | tf_op jit(solution)/shard_map/ppermute | solution.py:365
  54.2 4.2 %collective-permute-start.8 = (bf16[8,2,128,128]{3,2,1,0:T(8,128)(2,1)S(1)}, bf16[8,2,128,128]{3,2,1,0:T(8,128)(2,1)S(1)}, u32[]{:S(2)}, u32[]{:S(2)}) collective-permute-start(bf16[8,2,128,128]{3,2,1,0:T(8,128)(2,1)S(1)} %all-to-all-done.1.refs_3_), channel_id=1, source_target_pairs={{0,1},{1,0},{2,3},{3,2},{4,5},{5,4},{6,7},{7,6},{8,9},{9,8},{10,11... | collective-permute-start | bytes 1572872 | tf_op jit(solution)/shard_map/ppermute | solution.py:362
  54.2 25.8 %collective-permute-start.9 = (bf16[16,128,256]{2,1,0:T(8,128)(2,1)}, bf16[16,128,256]{2,1,0:T(8,128)(2,1)S(1)}, u32[]{:S(2)}, u32[]{:S(2)}) collective-permute-start(bf16[16,128,256]{2,1,0:T(8,128)(2,1)} %get-tuple-element.51.refs_5_), channel_id=1, source_target_pairs={{0,12},{4,0},{8,4},{12,8},{1,13},{5,1},{9,5},{13,9},{2,14},{6,2},{... | collective-permute-start | bytes 3145736 | tf_op jit(solution)/shard_map/ppermute | solution.py:365
  56.3 25.5 %collective-permute-start.10 = (bf16[16,128,256]{2,1,0:T(8,128)(2,1)}, bf16[16,128,256]{2,1,0:T(8,128)(2,1)S(1)}, u32[]{:S(2)}, u32[]{:S(2)}) collective-permute-start(bf16[16,128,256]{2,1,0:T(8,128)(2,1)} %get-tuple-element.52.refs_6_), channel_id=1, source_target_pairs={{0,2},{2,16},{16,18},{18,0},{1,3},{3,17},{17,19},{19,1},{4,6},{6,2... | collective-permute-start | bytes 3145736 | tf_op jit(solution)/shard_map/ppermute | solution.py:365
  77.9 23.9 %copy-start.1 = (s32[607]{0:T(1024)S(1)}, s32[607]{0:T(1024)}, u32[]{:S(2)}) copy-start(s32[607]{0:T(1024)} %get-tuple-element.49.refs_2_) | copy-start | bytes 7288
  77.9 23.9 %copy-start.4 = (s32[32]{0:T(128)S(1)}, s32[32]{0:T(128)}, u32[]{:S(2)}) copy-start(s32[32]{0:T(128)} %get-tuple-element.48.refs_1_) | copy-start | bytes 388
  77.9 23.7 %collective-permute-start.11 = (bf16[16,128,256]{2,1,0:T(8,128)(2,1)S(1)}, bf16[16,128,256]{2,1,0:T(8,128)(2,1)S(1)}, u32[]{:S(2)}, u32[]{:S(2)}) collective-permute-start(bf16[16,128,256]{2,1,0:T(8,128)(2,1)S(1)} %collective-permute-done.6.refs_7_), channel_id=1, source_target_pairs={{0,4},{4,8},{8,12},{12,0},{1,5},{5,9},{9,13},{13,1},{2,6},{6,10},{... | collective-permute-start | bytes 3145736 | tf_op jit(solution)/shard_map/ppermute | solution.py:365
  78.3 23.6 %collective-permute-start.12 = (bf16[16,128,256]{2,1,0:T(8,128)(2,1)S(1)}, bf16[16,128,256]{2,1,0:T(8,128)(2,1)S(1)}, u32[]{:S(2)}, u32[]{:S(2)}) collective-permute-start(bf16[16,128,256]{2,1,0:T(8,128)(2,1)S(1)} %collective-permute-done.7.refs_10_), channel_id=1, source_target_pairs={{0,18},{2,0},{16,2},{18,16},{1,19},{3,1},{17,3},{19,17},{4,22},{6,... | collective-permute-start | bytes 3145736 | tf_op jit(solution)/shard_map/ppermute | solution.py:365
  111.6 2.1 %collective-permute-start.14 = (bf16[8,2,128,128]{3,2,1,0:T(8,128)(2,1)S(1)}, bf16[8,2,128,128]{3,2,1,0:T(8,128)(2,1)S(1)}, u32[]{:S(2)}, u32[]{:S(2)}) collective-permute-start(bf16[8,2,128,128]{3,2,1,0:T(8,128)(2,1)S(1)} %get-tuple-element.74), channel_id=1, source_target_pairs={{0,1},{1,0},{2,3},{3,2},{4,5},{5,4},{6,7},{7,6},{8,9},{9,8},{10,11... | collective-permute-start | bytes 1572872 | tf_op jit(solution)/shard_map/ppermute | solution.py:381
  111.7 2.0 %collective-permute-start.13 = (f32[8,2,8,128]{3,2,1,0:T(8,128)S(1)}, f32[8,2,8,128]{3,2,1,0:T(8,128)S(1)}, u32[]{:S(2)}, u32[]{:S(2)}) collective-permute-start(f32[8,2,8,128]{3,2,1,0:T(8,128)S(1)} %get-tuple-element.73), channel_id=1, source_target_pairs={{0,1},{1,0},{2,3},{3,2},{4,5},{5,4},{6,7},{7,6},{8,9},{9,8},{10,11... | collective-permute-start | bytes 196616 | tf_op jit(solution)/shard_map/ppermute | solution.py:382
where the time goes:
time: 142 us; the launch traced here: 139 us
  Pallas kernels  49.2 us (35%)
  waiting for transfers between devices  31.6 us (22%)
  starting transfers between devices  29.5 us (21%)
  blocking collectives  23.7 us (17%)
  local copies, waits for them, and re-layouts  4.41 us (3%)
    pallas_call x3, Pallas kernels, attend(): pl.pallas_call(functools.partial(attend_kernel, blocks, first, last, move...  39 us
    all_to_all x1, blocking collectives, shards(): lax.all_to_all(o.astype(jnp.bfloat16), 'z', split_axis=0, concat_axis=0,...  23.7 us
    ppermute x12, waiting for transfers between devices, shift(): return lax.ppermute(value, axis, ring(4, d))  22.8 us
    ppermute x12, starting transfers between devices, shift(): return lax.ppermute(value, axis, ring(4, d))  16.8 us
    all_to_all x1, starting transfers between devices, shards(): kv_z = lax.all_to_all(kv_send, 'z', split_axis=0, concat_axis=0, tiled=True)  8.47 us
    all_to_all x1, waiting for transfers between devices, shards(): kv_z = lax.all_to_all(kv_send, 'z', split_axis=0, concat_axis=0, tiled=True)  7.34 us
    pallas_call x1, Pallas kernels, plan(): pl.pallas_call(functools.partial(plan_kernel, parts), out_shape=[jax.Shap...  6.89 us
    all_to_all x1, starting transfers between devices, shards(): q_own = lax.all_to_all(qt, 'z', split_axis=0, concat_axis=0, tiled=True)  3.63 us
  transfers between devices with their start and end apart: 17, of which 11 were waited for; matrix products, arithmetic and copies ran while one was open for 2% of the time, Pallas kernels for 27%

commit v1 on v0

--- a/solution.py
+++ b/solution.py
@@ -19,14 +19,14 @@
 NEVER = 1e30
 LOG2E_SCALE = math.log2(math.e) / math.sqrt(HD)
 SHIFTS = (0, -1, 1, 2)
-UNITS = ((8, False), (4, False), (2, False), (1, False), (1, True))
+UNITS = ((8, False), (4, False), (2, False), (1, True))
 WIDEST = UNITS[0][0]
 
 
 def layout(blocks):
     offsets = [len(UNITS) + 2]
     for wide, masked in UNITS:
-        most = blocks if wide == 8 else 8 * 3 if masked else 8
+        most = blocks if wide == 8 else 8 * 4 if masked else 8
         offsets.append(offsets[-1] + most)
     return offsets[:-1] + [offsets[-1], offsets[-1] + 8 * blocks, offsets[-1] + 16 * blocks + 8]
 
@@ -70,7 +70,7 @@
         *kinds, plain_b, mixed_b, _ = layout(blocks)
         for half in range(2):
             for n in range(wide):
-                d, e = far[n // 4], SHIFTS[n % 4]
+                d, e = far[n // 4] * (1 - 2 * core), SHIFTS[n % 4]
                 dx, dy = (e, d) if half == 0 else (d, e)
                 first = within((x + dx + 4) % 4, (y + dy + 4) % 4) + core * TILE
                 for p in range(4):
@@ -97,6 +97,9 @@
             plain_at, mixed_at = plain_b + plain, mixed_b + mixed
             left, more = p - plain_at, m - mixed_at
             for kind, (size, masked) in enumerate(UNITS):
+                if masked:
+                    out[mixed_at + more] = out[plain_at]
+                    more = more + left
                 at, count = (mixed_at, more) if masked else (plain_at, left)
                 n = count // size
 
@@ -110,7 +113,7 @@
                     mixed_at, more = at + n * size, count - n * size
                 else:
                     plain_at, left = at + n * size, count - n * size
-            return (p - plain_b, m - mixed_b, *counts)
+            return (p - plain_b, mixed_at - mixed_b, *counts)
 
         none = (jnp.int32(0),) * (2 + len(UNITS))
         counts = lax.fori_loop(0, 8, plane, none)[2:]
@@ -366,14 +369,20 @@
 
     xs, ys = ("xh", "xl"), "y"
     first, second = kv_z[:4], kv_z[4:]
-    near_a = [first] + [shift(first, xs, -d) for d in SHIFTS[1:]]
-    near_b = [second] + [shift(second, ys, -d) for d in SHIFTS[1:]]
+    near_a, near_b = [first] + [None] * 3, [second] + [None] * 3
+    for n in (3, 1, 2):
+        near_a[n] = shift(first, xs, -SHIFTS[n])
+        near_b[n] = shift(second, ys, -SHIFTS[n])
     part_a, part_b = pack(near_a, near_b)
-    a_up, a_down = shift(part_a, ys, 1), shift(part_a, ys, -1)
-    b_up, b_down = shift(part_b, xs, 1), shift(part_b, xs, -1)
+    def turn(value, axes, d):
+        pairs = [(2 * i + c, 2 * ((i + d - 2 * d * c) % 4) + c) for i in range(4) for c in range(2)]
+        return lax.ppermute(value, (*axes, "c"), pairs)
+
+    a_up, b_down = turn(part_a, ("y",), 1), turn(part_b, xs, -1)
+    a_down, b_up = turn(part_a, ("y",), -1), turn(part_b, xs, 1)
     qq, *state = attend(info, tables[0], lists[0], (q_own, q_other), None, [part_a, part_b], False, 4)
     a_up, b_down, qq, state = lax.optimization_barrier((a_up, b_down, qq, state))
-    a_far, b_far = shift(a_up, ys, 1), shift(b_down, xs, -1)
+    a_far, b_far = turn(a_up, ("y",), 1), turn(b_down, xs, -1)
     state = attend(info, tables[1], lists[1], None, [qq, *state], [a_up, a_down, b_up, b_down], False, 8)
     o_own, o_other, lse_own, lse_other = attend(
         info, tables[2], lists[2], None, [qq, *state], [a_far, b_far], True, 4)

time: 142 us -> 137 us (0.965); the launches traced: 139 us -> 138 us
  waiting for transfers between devices: 31.6 us -> 26 us
  Pallas kernels: 49.2 us -> 52.3 us
    ppermute x12 -> x6, waiting for transfers between devices: 22.8 us -> 9.02 us  [shift(): return lax.ppermute(value, axis, ring(4, d))]
    ppermute x0 -> x6, waiting for transfers between devices: none -> 8.89 us  [turn(): return lax.ppermute(value, (*axes, 'c'), pairs)]
    ppermute x12 -> x6, starting transfers between devices: 16.8 us -> 9.94 us  [shift(): return lax.ppermute(value, axis, ring(4, d))]
    ppermute x0 -> x6, starting transfers between devices: none -> 6.7 us  [turn(): return lax.ppermute(value, (*axes, 'c'), pairs)]
    pallas_call x3, Pallas kernels: 39 us -> 41.4 us  [attend(): pl.pallas_call(functools.partial(attend_kernel, blocks, first, last, move...]
  transfers between devices with their start and end apart: 17 -> 17, of which waited for: 11 -> 7; matrix products, arithmetic and copies ran while one was open for 2% -> 2% of each run, Pallas kernels for 27% -> 28%
where the time goes in v1:
time: 137 us; the launch traced here: 138 us
  Pallas kernels  52.3 us (38%)
  starting transfers between devices  29.3 us (21%)
  waiting for transfers between devices  26 us (19%)
  blocking collectives  24.5 us (18%)
  local copies, waits for them, and re-layouts  4.41 us (3%)
    pallas_call x3, Pallas kernels, attend(): pl.pallas_call(functools.partial(attend_kernel, blocks, first, last, move...  41.4 us
    all_to_all x1, blocking collectives, shards(): lax.all_to_all(o.astype(jnp.bfloat16), 'z', split_axis=0, concat_axis=0,...  24.5 us
    ppermute x6, starting transfers between devices, shift(): return lax.ppermute(value, axis, ring(4, d))  9.94 us
    ppermute x6, waiting for transfers between devices, shift(): return lax.ppermute(value, axis, ring(4, d))  9.02 us
    ppermute x6, waiting for transfers between devices, turn(): return lax.ppermute(value, (*axes, 'c'), pairs)  8.89 us
    all_to_all x1, starting transfers between devices, shards(): kv_z = lax.all_to_all(kv_send, 'z', split_axis=0, concat_axis=0, tiled=True)  8.47 us
    pallas_call x1, Pallas kernels, plan(): pl.pallas_call(functools.partial(plan_kernel, parts), out_shape=[jax.Shap...  7.61 us
    ppermute x6, starting transfers between devices, turn(): return lax.ppermute(value, (*axes, 'c'), pairs)  6.7 us
  transfers between devices with their start and end apart: 17, of which 7 were waited for; matrix products, arithmetic and copies ran while one was open for 2% of the time, Pallas kernels for 28%

profile of v1, /device:TPU:6, one launch (start us, length us, event | category | flops | bytes accessed | tf_op | source)
XLA Modules:
  0.0 137.6 jit_solution(5795329908676891655)
XLA Ops:
  0.0 1.8 %shard_map.46 = bf16[8,128,256]{2,1,0:T(8,128)(2,1)} custom-call(bf16[128,256]{1,0:T(8,128)(2,1)} %keys.1, bf16[128,256]{1,0:T(8,128)(2,1)} %values.1), custom_call_target="tpu_custom_call" | custom-call | tf_op jit(solution)/shard_map/pallas_call | solution.py:151
  1.8 8.5 %all-to-all-start = ((bf16[8,128,256]{2,1,0:T(8,128)(2,1)}), bf16[8,128,256]{2,1,0:T(8,128)(2,1)S(1)}, u32[]{:S(2)}, u32[]{:S(2)}) async-start(bf16[8,128,256]{2,1,0:T(8,128)(2,1)} %shard_map.46), calls=%async_computation | async-start | bytes 1048576 | tf_op jit(solution)/shard_map/all_to_all | solution.py:359
  10.3 1.4 %reshape.12 = bf16[128,2,4,2,128]{4,3,2,1,0:T(2,128)(2,1)S(1)} reshape(bf16[128,2048]{1,0:T(8,128)(2,1)} %param.4) | data formatting | bytes 1048576 | tf_op jit(solution)/shard_map/reshape | solution.py:360
  11.7 1.3 copy.5
  12.9 0.6 pad_add_fusion.spot
  13.5 7.6 %shard_map.47 = (s32[52]{0:T(128)}, s32[32]{0:T(128)}, s32[64]{0:T(128)}, s32[32]{0:T(128)}, s32[606]{0:T(1024)}, /*index=5*/s32[1150]{0:T(1024)}, s32[606]{0:T(1024)}) custom-call(s32[16]{0:T(128)} %lengths.1, s32[3]{0:T(128)} %pad_add_fusion.spot), custom_call_target="tpu_custom_call" | custom-call | tf_op jit(solution)/shard_map/pallas_call | solution.py:129
  21.1 6.6 %all-to-all-done = bf16[8,128,256]{2,1,0:T(8,128)(2,1)S(1)} async-done(((bf16[8,128,256]{2,1,0:T(8,128)(2,1)}), bf16[8,128,256]{2,1,0:T(8,128)(2,1)S(1)}, u32[]{:S(2)}, u32[]{:S(2)}) %all-to-all-start) | async-done | bytes 524320 | tf_op jit(solution)/shard_map/all_to_all | solution.py:359
  27.8 3.6 %all-to-all-start.1 = ((bf16[8,2,128,128]{3,2,1,0:T(8,128)(2,1)}), bf16[8,2,128,128]{3,2,1,0:T(8,128)(2,1)S(1)}, u32[]{:S(2)}, u32[]{:S(2)}) async-start(bf16[8,2,128,128]{3,2,1,0:T(8,128)(2,1)} %bitcast.1), calls=%async_computation.1 | async-start | bytes 1048576 | tf_op jit(solution)/shard_map/all_to_all | solution.py:364
  31.4 0.6 collective-permute-start
  32.0 1.5 %collective-permute-start.1 = (bf16[4,128,256]{2,1,0:T(8,128)(2,1)S(1)}, bf16[4,128,256]{2,1,0:T(8,128)(2,1)S(1)}, u32[]{:S(2)}, u32[]{:S(2)}) collective-permute-start(bf16[4,128,256]{2,1,0:T(8,128)(2,1)S(1)} %get-tuple-element.79.refs_0_), channel_id=1, source_target_pairs={{0,18},{2,0},{16,2},{18,16},{1,19},{3,1},{17,3},{19,17},{4,22},{6,... | collective-permute-start | bytes 786440 | tf_op jit(solution)/shard_map/ppermute | solution.py:368
  33.5 1.4 %collective-permute-start.2 = (bf16[4,128,256]{2,1,0:T(8,128)(2,1)S(1)}, bf16[4,128,256]{2,1,0:T(8,128)(2,1)S(1)}, u32[]{:S(2)}, u32[]{:S(2)}) collective-permute-start(bf16[4,128,256]{2,1,0:T(8,128)(2,1)S(1)} %get-tuple-element.79.refs_0_), channel_id=1, source_target_pairs={{0,16},{2,18},{16,0},{18,2},{1,17},{3,19},{17,1},{19,3},{4,20},{6,... | collective-permute-start | bytes 786440 | tf_op jit(solution)/shard_map/ppermute | solution.py:368
  34.9 1.6 %collective-permute-start.3 = (bf16[4,128,256]{2,1,0:T(8,128)(2,1)S(1)}, bf16[4,128,256]{2,1,0:T(8,128)(2,1)S(1)}, u32[]{:S(2)}, u32[]{:S(2)}) collective-permute-start(bf16[4,128,256]{2,1,0:T(8,128)(2,1)S(1)} %get-tuple-element.78.refs_4_), channel_id=1, source_target_pairs={{0,4},{4,8},{8,12},{12,0},{1,5},{5,9},{9,13},{13,1},{2,6},{6,10},{... | collective-permute-start | bytes 786440 | tf_op jit(solution)/shard_map/ppermute | solution.py:368
  36.5 1.7 %collective-permute-start.4 = (bf16[4,128,256]{2,1,0:T(8,128)(2,1)S(1)}, bf16[4,128,256]{2,1,0:T(8,128)(2,1)S(1)}, u32[]{:S(2)}, u32[]{:S(2)}) collective-permute-start(bf16[4,128,256]{2,1,0:T(8,128)(2,1)S(1)} %get-tuple-element.78.refs_4_), channel_id=1, source_target_pairs={{0,12},{4,0},{8,4},{12,8},{1,13},{5,1},{9,5},{13,9},{2,14},{6,2},{... | collective-permute-start | bytes 786440 | tf_op jit(solution)/shard_map/ppermute | solution.py:368
  38.2 2.5 %collective-permute-done.refs_1_ = bf16[4,128,256]{2,1,0:T(8,128)(2,1)S(1)} collective-permute-done((bf16[4,128,256]{2,1,0:T(8,128)(2,1)S(1)}, bf16[4,128,256]{2,1,0:T(8,128)(2,1)S(1)}, u32[]{:S(2)}, u32[]{:S(2)}) %collective-permute-start) | collective-permute-done | bytes 262176 | tf_op jit(solution)/shard_map/ppermute | solution.py:368
  40.7 3.2 %collective-permute-start.5 = (bf16[4,128,256]{2,1,0:T(8,128)(2,1)S(1)}, bf16[4,128,256]{2,1,0:T(8,128)(2,1)S(1)}, u32[]{:S(2)}, u32[]{:S(2)}) collective-permute-start(bf16[4,128,256]{2,1,0:T(8,128)(2,1)S(1)} %get-tuple-element.78.refs_4_), channel_id=1, source_target_pairs={{0,8},{4,12},{8,0},{12,4},{1,9},{5,13},{9,1},{13,5},{2,10},{6,14},... | collective-permute-start | bytes 786440 | tf_op jit(solution)/shard_map/ppermute | solution.py:368
  43.9 2.9 %collective-permute-done.1.refs_2_ = bf16[4,128,256]{2,1,0:T(8,128)(2,1)S(1)} collective-permute-done((bf16[4,128,256]{2,1,0:T(8,128)(2,1)S(1)}, bf16[4,128,256]{2,1,0:T(8,128)(2,1)S(1)}, u32[]{:S(2)}, u32[]{:S(2)}) %collective-permute-start.1) | collective-permute-done | bytes 262176 | tf_op jit(solution)/shard_map/ppermute | solution.py:368
  46.8 3.6 %collective-permute-done.5.refs_7_ = bf16[4,128,256]{2,1,0:T(8,128)(2,1)S(1)} collective-permute-done((bf16[4,128,256]{2,1,0:T(8,128)(2,1)S(1)}, bf16[4,128,256]{2,1,0:T(8,128)(2,1)S(1)}, u32[]{:S(2)}, u32[]{:S(2)}) %collective-permute-start.5) | collective-permute-done | bytes 262176 | tf_op jit(solution)/shard_map/ppermute | solution.py:368
  50.4 1.5 %shard_map.48 = (bf16[16,128,256]{2,1,0:T(8,128)(2,1)}, bf16[16,128,256]{2,1,0:T(8,128)(2,1)}) custom-call(bf16[4,128,256]{2,1,0:T(8,128)(2,1)S(1)} %get-tuple-element.79.refs_0_, bf16[4,128,256]{2,1,0:T(8,128)(2,1)S(1)} %collective-permute-done.refs_1_, bf16[4,128,256]{2,1,0:T(8,128)(2,1)S(1)} %collective-permute-done.1.refs_2_, ...), custom_call_target="tpu_custom_call" | custom-call | tf_op jit(solution)/shard_map/pallas_call | solution.py:171
  51.9 1.1 collective-permute-start.6
  53.0 1.1 collective-permute-start.7
  54.2 2.1 %collective-permute-start.9 = (bf16[16,128,256]{2,1,0:T(8,128)(2,1)}, bf16[16,128,256]{2,1,0:T(8,128)(2,1)S(1)}, u32[]{:S(2)}, u32[]{:S(2)}) collective-permute-start(bf16[16,128,256]{2,1,0:T(8,128)(2,1)} %get-tuple-element.51.refs_5_), channel_id=1, source_target_pairs={{0,12},{1,5},{4,0},{5,9},{8,4},{9,13},{12,8},{13,1},{2,14},{3,7},{... | collective-permute-start | bytes 3145736 | tf_op jit(solution)/shard_map/ppermute | solution.py:379
  56.3 2.1 %collective-permute-start.10 = (bf16[16,128,256]{2,1,0:T(8,128)(2,1)}, bf16[16,128,256]{2,1,0:T(8,128)(2,1)S(1)}, u32[]{:S(2)}, u32[]{:S(2)}) collective-permute-start(bf16[16,128,256]{2,1,0:T(8,128)(2,1)} %get-tuple-element.52.refs_6_), channel_id=1, source_target_pairs={{0,2},{1,19},{2,16},{3,1},{16,18},{17,3},{18,0},{19,17},{4,6},{5,2... | collective-permute-start | bytes 3145736 | tf_op jit(solution)/shard_map/ppermute | solution.py:379
  58.4 12.6 %shard_map.49 = (bf16[8,256,512]{2,1,0:T(8,128)(2,1)S(1)}, f32[8,128,512]{2,1,0:T(8,128)S(1)}, f32[8,8,512]{2,1,0:T(8,128)S(1)}, f32[8,8,512]{2,1,0:T(8,128)S(1)}) custom-call(s32[52]{0:T(128)S(1)} %copy-done.3, s32[32]{0:T(128)S(1)} %copy-done.6, s32[606]{0:T(1024)S(1)} %copy-done.2, bf16[8,2,128,128]{3,2,1,0:T(8,128)(2,1)S(1)} %all-to-all-done.1.refs_3_, ...), custom_call_target="tpu_custom_call" | custom-call | flops 4000000000 | bytes 8388608 | tf_op jit(solution)/shard_map/pallas_call | solution.py:332
  71.0 6.5 %collective-permute-done.6.refs_7_ = bf16[16,128,256]{2,1,0:T(8,128)(2,1)S(1)} collective-permute-done((bf16[16,128,256]{2,1,0:T(8,128)(2,1)}, bf16[16,128,256]{2,1,0:T(8,128)(2,1)S(1)}, u32[]{:S(2)}, u32[]{:S(2)}) %collective-permute-start.6) | collective-permute-done | bytes 1048608 | tf_op jit(solution)/shard_map/ppermute | solution.py:379
  77.5 2.4 %collective-permute-done.7.refs_10_ = bf16[16,128,256]{2,1,0:T(8,128)(2,1)S(1)} collective-permute-done((bf16[16,128,256]{2,1,0:T(8,128)(2,1)}, bf16[16,128,256]{2,1,0:T(8,128)(2,1)S(1)}, u32[]{:S(2)}, u32[]{:S(2)}) %collective-permute-start.7) | collective-permute-done | bytes 1048608 | tf_op jit(solution)/shard_map/ppermute | solution.py:379
  80.1 17.4 %shard_map.50 = (f32[8,128,512]{2,1,0:T(8,128)S(1)}, f32[8,8,512]{2,1,0:T(8,128)S(1)}, f32[8,8,512]{2,1,0:T(8,128)S(1)}) custom-call(s32[52]{0:T(128)S(1)} %copy-done.3, s32[64]{0:T(128)S(1)} %copy-done.5, s32[1150]{0:T(1024)S(1)} %copy-done, bf16[8,256,512]{2,1,0:T(8,128)(2,1)S(1)} %get-tuple-element.60.refs_3_, ...), custom_call_target="tpu_custom_call" | custom-call | flops 8000000000 | bytes 8388608 | tf_op jit(solution)/shard_map/pallas_call | solution.py:332
  97.6 11.4 %shard_map.51 = (bf16[8,2,128,128]{3,2,1,0:T(8,128)(2,1)S(1)}, bf16[8,2,128,128]{3,2,1,0:T(8,128)(2,1)S(1)}, f32[8,2,8,128]{3,2,1,0:T(8,128)S(1)}, f32[8,2,8,128]{3,2,1,0:T(8,128)S(1)}) custom-call(s32[52]{0:T(128)S(1)} %copy-done.3, s32[32]{0:T(128)S(1)} %copy-done.4, s32[606]{0:T(1024)S(1)} %copy-done.1, ...), custom_call_target="tpu_custom_call" | custom-call | flops 4000000000 | bytes 8388608 | tf_op jit(solution)/shard_map/pallas_call | solution.py:332
  109.0 0.3 collective-permute-start.14
  109.6 1.5 %collective-permute-done.13 = f32[8,2,8,128]{3,2,1,0:T(8,128)S(1)} collective-permute-done((f32[8,2,8,128]{3,2,1,0:T(8,128)S(1)}, f32[8,2,8,128]{3,2,1,0:T(8,128)S(1)}, u32[]{:S(2)}, u32[]{:S(2)}) %collective-permute-start.13) | collective-permute-done | bytes 65568 | tf_op jit(solution)/shard_map/ppermute | solution.py:391
  111.4 24.5 %all_to_all.15 = bf16[8,2,128,128]{3,2,1,0:T(8,128)(2,1)S(1)} all-to-all(bf16[8,2,128,128]{3,2,1,0:T(8,128)(2,1)S(1)} %divide_convert_fusion), channel_id=1, replica_groups=mesh['z'=8,'xh'=2,'y'=4,'xl'=2,'c'=2] {'z'}, dimensions={0} | all-to-all | bytes 1048576 | tf_op jit(solution)/shard_map/all_to_all | solution.py:396
  135.9 0.5 copy.6
  136.4 1.2 reshape.15
  (31 shorter events, 0.9 us)
Async XLA Ops:
  1.8 26.0 %all-to-all-start = ((bf16[8,128,256]{2,1,0:T(8,128)(2,1)}), bf16[8,128,256]{2,1,0:T(8,128)(2,1)S(1)}, u32[]{:S(2)}, u32[]{:S(2)}) async-start(bf16[8,128,256]{2,1,0:T(8,128)(2,1)} %shard_map.46), calls=%async_computation | async-start | bytes 1048576 | tf_op jit(solution)/shard_map/all_to_all | solution.py:359
  27.7 30.6 %copy-start.2 = (s32[606]{0:T(1024)S(1)}, s32[606]{0:T(1024)}, u32[]{:S(2)}) copy-start(s32[606]{0:T(1024)} %get-tuple-element.54.refs_2_) | copy-start | bytes 7276
  27.7 30.6 %copy-start.3 = (s32[52]{0:T(128)S(1)}, s32[52]{0:T(128)}, u32[]{:S(2)}) copy-start(s32[52]{0:T(128)} %get-tuple-element.47.refs_0_) | copy-start | bytes 628
  27.8 30.6 %copy-start.6 = (s32[32]{0:T(128)S(1)}, s32[32]{0:T(128)}, u32[]{:S(2)}) copy-start(s32[32]{0:T(128)} %get-tuple-element.53.refs_1_) | copy-start | bytes 388
  27.8 26.4 %all-to-all-start.1 = ((bf16[8,2,128,128]{3,2,1,0:T(8,128)(2,1)}), bf16[8,2,128,128]{3,2,1,0:T(8,128)(2,1)S(1)}, u32[]{:S(2)}, u32[]{:S(2)}) async-start(bf16[8,2,128,128]{3,2,1,0:T(8,128)(2,1)} %bitcast.1), calls=%async_computation.1 | async-start | bytes 1048576 | tf_op jit(solution)/shard_map/all_to_all | solution.py:364
  31.4 9.2 %collective-permute-start = (bf16[4,128,256]{2,1,0:T(8,128)(2,1)S(1)}, bf16[4,128,256]{2,1,0:T(8,128)(2,1)S(1)}, u32[]{:S(2)}, u32[]{:S(2)}) collective-permute-start(bf16[4,128,256]{2,1,0:T(8,128)(2,1)S(1)} %get-tuple-element.79.refs_0_), channel_id=1, source_target_pairs={{0,2},{2,16},{16,18},{18,0},{1,3},{3,17},{17,19},{19,1},{4,6},{6,2... | collective-permute-start | bytes 786440 | tf_op jit(solution)/shard_map/ppermute | solution.py:368
  32.0 14.8 %collective-permute-start.1 = (bf16[4,128,256]{2,1,0:T(8,128)(2,1)S(1)}, bf16[4,128,256]{2,1,0:T(8,128)(2,1)S(1)}, u32[]{:S(2)}, u32[]{:S(2)}) collective-permute-start(bf16[4,128,256]{2,1,0:T(8,128)(2,1)S(1)} %get-tuple-element.79.refs_0_), channel_id=1, source_target_pairs={{0,18},{2,0},{16,2},{18,16},{1,19},{3,1},{17,3},{19,17},{4,22},{6,... | collective-permute-start | bytes 786440 | tf_op jit(solution)/shard_map/ppermute | solution.py:368
  33.5 13.2 %collective-permute-start.2 = (bf16[4,128,256]{2,1,0:T(8,128)(2,1)S(1)}, bf16[4,128,256]{2,1,0:T(8,128)(2,1)S(1)}, u32[]{:S(2)}, u32[]{:S(2)}) collective-permute-start(bf16[4,128,256]{2,1,0:T(8,128)(2,1)S(1)} %get-tuple-element.79.refs_0_), channel_id=1, source_target_pairs={{0,16},{2,18},{16,0},{18,2},{1,17},{3,19},{17,1},{19,3},{4,20},{6,... | collective-permute-start | bytes 786440 | tf_op jit(solution)/shard_map/ppermute | solution.py:368
  34.9 11.8 %collective-permute-start.3 = (bf16[4,128,256]{2,1,0:T(8,128)(2,1)S(1)}, bf16[4,128,256]{2,1,0:T(8,128)(2,1)S(1)}, u32[]{:S(2)}, u32[]{:S(2)}) collective-permute-start(bf16[4,128,256]{2,1,0:T(8,128)(2,1)S(1)} %get-tuple-element.78.refs_4_), channel_id=1, source_target_pairs={{0,4},{4,8},{8,12},{12,0},{1,5},{5,9},{9,13},{13,1},{2,6},{6,10},{... | collective-permute-start | bytes 786440 | tf_op jit(solution)/shard_map/ppermute | solution.py:368
  36.5 10.3 %collective-permute-start.4 = (bf16[4,128,256]{2,1,0:T(8,128)(2,1)S(1)}, bf16[4,128,256]{2,1,0:T(8,128)(2,1)S(1)}, u32[]{:S(2)}, u32[]{:S(2)}) collective-permute-start(bf16[4,128,256]{2,1,0:T(8,128)(2,1)S(1)} %get-tuple-element.78.refs_4_), channel_id=1, source_target_pairs={{0,12},{4,0},{8,4},{12,8},{1,13},{5,1},{9,5},{13,9},{2,14},{6,2},{... | collective-permute-start | bytes 786440 | tf_op jit(solution)/shard_map/ppermute | solution.py:368
  40.7 9.7 %collective-permute-start.5 = (bf16[4,128,256]{2,1,0:T(8,128)(2,1)S(1)}, bf16[4,128,256]{2,1,0:T(8,128)(2,1)S(1)}, u32[]{:S(2)}, u32[]{:S(2)}) collective-permute-start(bf16[4,128,256]{2,1,0:T(8,128)(2,1)S(1)} %get-tuple-element.78.refs_4_), channel_id=1, source_target_pairs={{0,8},{4,12},{8,0},{12,4},{1,9},{5,13},{9,1},{13,5},{2,10},{6,14},... | collective-permute-start | bytes 786440 | tf_op jit(solution)/shard_map/ppermute | solution.py:368
  51.9 25.6 %collective-permute-start.6 = (bf16[16,128,256]{2,1,0:T(8,128)(2,1)}, bf16[16,128,256]{2,1,0:T(8,128)(2,1)S(1)}, u32[]{:S(2)}, u32[]{:S(2)}) collective-permute-start(bf16[16,128,256]{2,1,0:T(8,128)(2,1)} %get-tuple-element.51.refs_5_), channel_id=1, source_target_pairs={{0,4},{1,13},{4,8},{5,1},{8,12},{9,5},{12,0},{13,9},{2,6},{3,15},{... | collective-permute-start | bytes 3145736 | tf_op jit(solution)/shard_map/ppermute | solution.py:379
  53.0 27.1 %copy-start = (s32[1150]{0:T(1024)S(1)}, s32[1150]{0:T(1024)}, u32[]{:S(2)}) copy-start(s32[1150]{0:T(1024)} %get-tuple-element.62.refs_2_) | copy-start | bytes 13804
  53.0 27.1 %copy-start.5 = (s32[64]{0:T(128)S(1)}, s32[64]{0:T(128)}, u32[]{:S(2)}) copy-start(s32[64]{0:T(128)} %get-tuple-element.61.refs_1_) | copy-start | bytes 772
  53.0 26.8 %collective-permute-start.7 = (bf16[16,128,256]{2,1,0:T(8,128)(2,1)}, bf16[16,128,256]{2,1,0:T(8,128)(2,1)S(1)}, u32[]{:S(2)}, u32[]{:S(2)}) collective-permute-start(bf16[16,128,256]{2,1,0:T(8,128)(2,1)} %get-tuple-element.52.refs_6_), channel_id=1, source_target_pairs={{0,18},{1,3},{2,0},{3,17},{16,2},{17,19},{18,16},{19,1},{4,22},{5,... | collective-permute-start | bytes 3145736 | tf_op jit(solution)/shard_map/ppermute | solution.py:379
  54.2 4.2 %collective-permute-start.8 = (bf16[8,2,128,128]{3,2,1,0:T(8,128)(2,1)S(1)}, bf16[8,2,128,128]{3,2,1,0:T(8,128)(2,1)S(1)}, u32[]{:S(2)}, u32[]{:S(2)}) collective-permute-start(bf16[8,2,128,128]{3,2,1,0:T(8,128)(2,1)S(1)} %all-to-all-done.1.refs_3_), channel_id=1, source_target_pairs={{0,1},{1,0},{2,3},{3,2},{4,5},{5,4},{6,7},{7,6},{8,9},{9,8},{10,11... | collective-permute-start | bytes 1572872 | tf_op jit(solution)/shard_map/ppermute | solution.py:365
  54.2 25.9 %collective-permute-start.9 = (bf16[16,128,256]{2,1,0:T(8,128)(2,1)}, bf16[16,128,256]{2,1,0:T(8,128)(2,1)S(1)}, u32[]{:S(2)}, u32[]{:S(2)}) collective-permute-start(bf16[16,128,256]{2,1,0:T(8,128)(2,1)} %get-tuple-element.51.refs_5_), channel_id=1, source_target_pairs={{0,12},{1,5},{4,0},{5,9},{8,4},{9,13},{12,8},{13,1},{2,14},{3,7},{... | collective-permute-start | bytes 3145736 | tf_op jit(solution)/shard_map/ppermute | solution.py:379
  56.3 23.8 %collective-permute-start.10 = (bf16[16,128,256]{2,1,0:T(8,128)(2,1)}, bf16[16,128,256]{2,1,0:T(8,128)(2,1)S(1)}, u32[]{:S(2)}, u32[]{:S(2)}) collective-permute-start(bf16[16,128,256]{2,1,0:T(8,128)(2,1)} %get-tuple-element.52.refs_6_), channel_id=1, source_target_pairs={{0,2},{1,19},{2,16},{3,1},{16,18},{17,3},{18,0},{19,17},{4,6},{5,2... | collective-permute-start | bytes 3145736 | tf_op jit(solution)/shard_map/ppermute | solution.py:379
  79.8 17.7 %copy-start.1 = (s32[606]{0:T(1024)S(1)}, s32[606]{0:T(1024)}, u32[]{:S(2)}) copy-start(s32[606]{0:T(1024)} %get-tuple-element.49.refs_2_) | copy-start | bytes 7276
  79.9 17.7 %copy-start.4 = (s32[32]{0:T(128)S(1)}, s32[32]{0:T(128)}, u32[]{:S(2)}) copy-start(s32[32]{0:T(128)} %get-tuple-element.48.refs_1_) | copy-start | bytes 388
  79.9 17.7 %collective-permute-start.11 = (bf16[16,128,256]{2,1,0:T(8,128)(2,1)S(1)}, bf16[16,128,256]{2,1,0:T(8,128)(2,1)S(1)}, u32[]{:S(2)}, u32[]{:S(2)}) collective-permute-start(bf16[16,128,256]{2,1,0:T(8,128)(2,1)S(1)} %collective-permute-done.6.refs_7_), channel_id=1, source_target_pairs={{0,4},{1,13},{4,8},{5,1},{8,12},{9,5},{12,0},{13,9},{2,6},{3,15},{... | collective-permute-start | bytes 3145736 | tf_op jit(solution)/shard_map/ppermute | solution.py:379
  79.9 17.7 %collective-permute-start.12 = (bf16[16,128,256]{2,1,0:T(8,128)(2,1)S(1)}, bf16[16,128,256]{2,1,0:T(8,128)(2,1)S(1)}, u32[]{:S(2)}, u32[]{:S(2)}) collective-permute-start(bf16[16,128,256]{2,1,0:T(8,128)(2,1)S(1)} %collective-permute-done.7.refs_10_), channel_id=1, source_target_pairs={{0,18},{1,3},{2,0},{3,17},{16,2},{17,19},{18,16},{19,1},{4,22},{5,... | collective-permute-start | bytes 3145736 | tf_op jit(solution)/shard_map/ppermute | solution.py:379
  109.0 2.1 %collective-permute-start.14 = (bf16[8,2,128,128]{3,2,1,0:T(8,128)(2,1)S(1)}, bf16[8,2,128,128]{3,2,1,0:T(8,128)(2,1)S(1)}, u32[]{:S(2)}, u32[]{:S(2)}) collective-permute-start(bf16[8,2,128,128]{3,2,1,0:T(8,128)(2,1)S(1)} %get-tuple-element.74), channel_id=1, source_target_pairs={{0,1},{1,0},{2,3},{3,2},{4,5},{5,4},{6,7},{7,6},{8,9},{9,8},{10,11... | collective-permute-start | bytes 1572872 | tf_op jit(solution)/shard_map/ppermute | solution.py:390
  109.3 1.8 %collective-permute-start.13 = (f32[8,2,8,128]{3,2,1,0:T(8,128)S(1)}, f32[8,2,8,128]{3,2,1,0:T(8,128)S(1)}, u32[]{:S(2)}, u32[]{:S(2)}) collective-permute-start(f32[8,2,8,128]{3,2,1,0:T(8,128)S(1)} %get-tuple-element.73), channel_id=1, source_target_pairs={{0,1},{1,0},{2,3},{3,2},{4,5},{5,4},{6,7},{7,6},{8,9},{9,8},{10,11... | collective-permute-start | bytes 196616 | tf_op jit(solution)/shard_map/ppermute | solution.py:391
